TPU v7x, 32 devices: a whole 2x2x4 slice. The times are simulated.
32 devices in a mesh: front: 8 (over z, x), col: 4 (over y, core).
Axes of the slice: x: 2, y: 2, z: 4, core: 2. Of those that a mesh axis runs over, the one named last changes fastest.
Arguments:
- leaf_load: bfloat16 [8192, 2048], P('front', 'col'), may hold values from -6 to 6
- leaf_inverse: bfloat16 [8192, 1024], P(('front', 'col')), may hold values from -0.1875 to 0.1875
- leaf_coupling: bfloat16 [4096, 1024], P('front'), may hold values from -0.1875 to 0.1875
- leaf_rowmap: int32 [8, 512], P('front'), may hold values from 0 to 511, each once within a row
- load_first: bfloat16 [2048, 2048], P('front', 'col'), may hold values from -6 to 6
- load_second: bfloat16 [1024, 2048], P('front', 'col'), may hold values from -6 to 6
- load_third: bfloat16 [512, 2048], P('front', 'col'), may hold values from -6 to 6
- inverse_first: bfloat16 [2048, 512], P('front'), may hold values from -0.15625 to 0.15625
- inverse_second: bfloat16 [1024, 512], P('front'), may hold values from -0.15625 to 0.15625
- inverse_third: bfloat16 [512, 512], P('front'), may hold values from -0.15625 to 0.15625
- coupling_first: bfloat16 [512, 2048], P(None, 'front'), may hold values from -0.25 to 0.25
- coupling_second: bfloat16 [512, 1024], P(None, 'front'), may hold values from -0.25 to 0.25
- rowmap_first: int32 [4, 512], replicated, may hold values from 0 to 511, each once within a row
- rowmap_second: int32 [2, 512], replicated, may hold values from 0 to 511, each once within a row
- surface_coupling: bfloat16 [24, 1024, 1024], P('front'), may hold values from -0.125 to 0.125
- neighbor_tiles: int32 [8, 2], replicated, may hold values from 0 to 7, as said below
Outputs:
- volume_solution: bfloat16 [8192, 2048], P('front', 'col')
- surface_tiles: bfloat16 [8192, 2048], P('front', 'col')
- solution_first: bfloat16 [2048, 2048], P('front', 'col')
- solution_second: bfloat16 [1024, 2048], P('front', 'col')
- solution_third: bfloat16 [512, 2048], P('front', 'col')
Inputs may be any that keep to these rules, and one draw needn't show every extreme that they name: Each row of leaf_rowmap is a permutation of the 512 separator rows. Each row of rowmap_first is a permutation of the 512 separator rows. Each row of rowmap_second is a permutation of the 512 separator rows. `neighbor_tiles`: row f names two different tiles, neither equal to f, each within 2 of f; counting each front's own tile, every tile receives 1 to 5 contributions, and some tile receives 5.
All inputs are finite; a program needn't handle non-finite values.
Results may differ from a plain program's by a relative error of at most 0.015.
Values may be sent and summed in bfloat16 or wider, within the bound.
A program may use at most 128 MiB of HBM per device.

v0:
```python
import functools

import jax
import jax.numpy as jnp
from jax import lax
from jax.experimental import pallas as pl
from jax.experimental.pallas import tpu as pltpu
from jax.sharding import PartitionSpec as P

BF = jnp.bfloat16
F32 = jnp.float32
MESH = pl.DeviceIdType.MESH
X, Z_ON, Z_BACK, DIAGONAL = range(4)


def mm(a, b):
    return jnp.dot(a, b, preferred_element_type=F32)


def tmm(a, b):
    return lax.dot_general(a, b, (((0,), (0,)), ((), ())), preferred_element_type=F32)


def flip(x, bit):
    return x + bit * (1 - 2 * ((x // bit) % 2))


def kernel(
    n, b_hbm, g_ref, c_hbm, map0, l1, l2, l3, i1, i2, i3, d_ref, e_ref, map1, map2, tile_ref, a_hbm,
    vol, tiles, o1, o2, o3,
    gf, ct, start, part, w1, w2, w3, l1f, l2f, l3f,
    b_ref, c_ref, give1, x1, y1, p2, x2, y2, p3, x3, s3, s2, s1, o3s, o2s, pull, value, av, stage, got, bent,
    send_sem, recv_sem, tile_send, tile_recv, load_sem,
):
    f = lax.axis_index("front")
    c = lax.axis_index("col")
    core = c % 2
    ca, cb = flip(c, 1), flip(c, 2)
    cd = flip(ca, 2)
    b0, b1 = f % 2, (f // 2) % 2
    fx, fy, fz = flip(f, 1), flip(f, 2), flip(f, 4)
    sep = l1f.shape[0]
    panel = b_ref.shape[1]
    half, quarter = panel // 2, panel // 4
    block = g_ref.shape[0]
    r1, r2, r3 = i1.shape[0], i2.shape[0], i3.shape[0]

    def cols(at, size):
        return pl.ds(pl.multiple_of(at, 128), size)

    def rows(at, size):
        return pl.ds(pl.multiple_of(at, 16), size)

    def half_of(g):
        return cols((g % 2) * half, half)

    copies = []

    def send(src, dst, **where):
        i = len(copies)
        copy = pltpu.make_async_remote_copy(
            src_ref=src, dst_ref=dst, send_sem=send_sem.at[i], recv_sem=recv_sem.at[i],
            device_id=where, device_id_type=MESH,
        )
        copies.append(copy)
        copy.start()
        return copy

    loads = [
        pltpu.make_async_copy(src, dst, load_sem.at[i])
        for i, (src, dst) in enumerate(((b_hbm, b_ref), (c_hbm, c_ref), (a_hbm, av)))
    ]
    for load in loads:
        load.start()

    barrier = pltpu.get_barrier_semaphore()
    for other in (ca, cb):
        pl.semaphore_signal(barrier, inc=1, device_id={"col": other}, device_id_type=MESH)
    for other in (fx, fy, fz):
        pl.semaphore_signal(barrier, inc=1, device_id={"front": other}, device_id_type=MESH)
    ahead = f + 2 * (2 * b0 - 1)
    behind = f - 2 * (2 * b0 - 1)
    has_ahead = jnp.logical_and(ahead >= 0, ahead < n)
    has_behind = jnp.logical_and(behind >= 0, behind < n)
    for ok, other in ((has_ahead, ahead), (has_behind, behind)):

        @pl.when(ok)
        def _(other=other):
            pl.semaphore_signal(barrier, inc=1, device_id={"front": other}, device_id_type=MESH)
    count = 5 + has_ahead.astype(jnp.int32) + has_behind.astype(jnp.int32)
    pl.semaphore_wait(barrier, count)

    own_rows = rows(c * block, block)
    g_near = send(g_ref, gf.at[own_rows], col=ca)
    piece = block // 2
    g_far = [
        send(g_ref.at[pl.ds(k * piece, piece)], gf.at[rows(c * block + k * piece, piece)], col=cb)
        for k in range(2)
    ]

    lines = lax.broadcasted_iota(jnp.int32, (sep, sep), 0)

    def chooser(row):
        return (lines == row).astype(F32).astype(BF)

    me1, me2, me3 = f % 2, f % 4, f % 8
    pair2, pair3, four3 = me2 - b0, me3 - b0, (me3 // 4) * 4
    in1, in2, in3 = rows(core * r1, r1), rows(core * r2, r2), rows(core * (r3 // 2), r3 // 2)
    w2[me2, 0:r2] = i2[...]
    w2[me2, r2 : 2 * r2] = tmm(e_ref[...], chooser(map2[pl.ds(f // 4, 1), :])).astype(BF)
    w3[me3] = i3[...]
    w2_x = send(w2.at[me2, in2], w2.at[me2, in2], front=fx)
    l2_x = send(l2.at[:, half_of(fx)], l2f.at[rows(me2 * r2, r2)], front=fx)
    w3_x = send(w3.at[me3, in3], w3.at[me3, in3], front=fx)
    l3_x = send(l3.at[:, half_of(fx)], l3f.at[rows(me3 * r3, r3)], front=fx)
    w1[me1, 0:r1] = i1[...]
    w1[me1, r1 : 2 * r1] = tmm(d_ref[...], chooser(map1[pl.ds(f // 2, 1), :])).astype(BF)
    w1_copy = send(w1.at[me1, in1], w1.at[me1, in1], front=fx)
    l1_copy = send(l1.at[:, half_of(fx)], l1f.at[rows(b0 * r1, r1)], front=fx)
    gf[own_rows] = g_ref[...]
    l1f[rows(b0 * r1, r1)] = l1[:, half_of(f)]
    l2f[rows(me2 * r2, r2)] = l2[:, half_of(f)]
    l3f[rows(me3 * r3, r3)] = l3[:, half_of(f)]

    @pl.when(jnp.logical_not(has_behind))
    def _():
        got[:, Z_ON] = jnp.zeros((2,) + got.shape[2:], BF)
        bent[...] = jnp.zeros(bent.shape, BF)

    @pl.when(jnp.logical_not(has_ahead))
    def _():
        got[:, Z_BACK] = jnp.zeros((2,) + got.shape[2:], BF)

    loads[1].wait()
    ct[...] = tmm(c_ref[...], chooser(map0[...])).astype(BF)

    def leaf(slot, first=False):
        at = rows(slot * block, block)
        solved = mm(gf[at], b_ref[...]).astype(BF)
        start[at] = solved
        term = tmm(ct[at], solved)
        part[...] = term if first else part[...] + term

    loads[0].wait()
    leaf(c, True)
    g_near.wait_recv()
    leaf(ca)
    for copy in (w2_x, l2_x, w3_x, l3_x):
        copy.wait_recv()
    two = w2.at[pl.ds(pair2, 2), in2]
    w2_y = send(two, two, front=fy)
    two = l2f.at[rows(pair2 * r2, 2 * r2)]
    l2_y = send(two, two, front=fy)
    two = w3.at[pl.ds(pair3, 2), in3]
    w3_y = send(two, two, front=fy)
    two = l3f.at[rows(pair3 * r3, 2 * r3)]
    l3_y = send(two, two, front=fy)
    g_pass = []
    for k in range(2):
        g_far[k].wait_recv()
        at = rows(cb * block + k * piece, piece)
        g_pass.append(send(gf.at[at], gf.at[at], col=ca))
    one = w2.at[flip(me2, 1), in2]
    w2_pass = [send(one, one, col=ca)]
    one = w3.at[flip(me3, 1), in3]
    w3_pass = [send(one, one, col=ca)]
    leaf(cb)
    w1_copy.wait_recv()
    one = w1.at[1 - me1, in1]
    w1_pass = send(one, one, col=ca)
    for k in range(2):
        g_pass[k].wait_recv()
    leaf(cd)

    def joined(w, at, size):
        return jnp.concatenate([w[m, at : at + size] for m in range(w.shape[0])], axis=0)

    def in_half(k):
        return pl.ds(k * quarter, quarter)

    def in_panel(which, k):
        return cols(which * half + k * quarter, quarter)

    x1_copies = []
    for k in range(2):
        give1[k] = part[:, in_panel(1 - b0, k)].astype(BF)
        x1_copies.append(send(give1.at[k], x1.at[k], front=fx))
    for copy in (w2_y, w3_y, l3_y):
        copy.wait_recv()
    four = w3.at[pl.ds(four3, 4), in3]
    w3_z = send(four, four, front=fz)
    four = l3f.at[rows(four3 * r3, 4 * r3)]
    l3_z = send(four, four, front=fz)
    two = w2.at[pl.ds(2 - pair2, 2), in2]
    w2_pass.append(send(two, two, col=ca))
    two = w3.at[pl.ds(four3 + 2 - (pair3 - four3), 2), in3]
    w3_pass.append(send(two, two, col=ca))
    l1_copy.wait_recv()
    w1_pass.wait_recv()
    x2_copies = []
    for k in range(2):
        x1_copies[k].wait_recv()
        rhs = l1f[:, in_half(k)].astype(F32) - part[:, in_panel(b0, k)] - x1[k].astype(F32)
        y1[k] = mm(joined(w1, 0, r1), rhs.astype(BF)).astype(BF)
        p2[k] = tmm(joined(w1, r1, r1), y1[k]).astype(BF)
        x2_copies.append(send(p2.at[k], x2.at[k], front=fy))
    for copy in [l2_y] + w2_pass:
        copy.wait_recv()
    x3_copies = []
    for k in range(2):
        x2_copies[k].wait_recv()
        rhs = l2f[:, in_half(k)].astype(F32) - p2[k].astype(F32) - x2[k].astype(F32)
        y2[k] = mm(joined(w2, 0, r2), rhs.astype(BF)).astype(BF)
        p3[k] = tmm(joined(w2, r2, r2), y2[k]).astype(BF)
        x3_copies.append(send(p3.at[k], x3.at[k], front=fz))
    w3_z.wait_recv()
    four = w3.at[pl.ds(4 - four3, 4), in3]
    w3_pass.append(send(four, four, col=ca))
    for copy in [l3_z] + w3_pass:
        copy.wait_recv()

    s1_copies = []
    for k in range(2):
        x3_copies[k].wait_recv()
        rhs = l3f[:, in_half(k)].astype(F32) - p3[k].astype(F32) - x3[k].astype(F32)
        top = mm(joined(w3, 0, r3), rhs.astype(BF)).astype(BF)
        s3[:, in_half(k)] = top
        pull2 = mm(joined(w2, r2, r2), top).astype(BF)
        second = (y2[k].astype(F32) - mm(joined(w2, 0, r2), pull2)).astype(BF)
        s2[:, in_half(k)] = second
        pull1 = mm(joined(w1, r1, r1), second).astype(BF)
        s1[k, b0] = (y1[k].astype(F32) - mm(joined(w1, 0, r1), pull1)).astype(BF)
        s1_copies.append(send(s1.at[k, b0], s1.at[k, b0], front=fx))
    o3_copy = send(s3.at[rows((fx % 8) * r3, r3)], o3s.at[b0], front=fx)
    o2_copy = send(s2.at[rows((fx % 4) * r2, r2)], o2s.at[b0], front=fx)
    loads[2].wait()

    chunk = block
    chunks = gf.shape[0] // chunk
    tile_chunks = got.shape[2] // chunk
    aimed = jnp.sum(
        jnp.where(
            lax.broadcasted_iota(jnp.int32, tile_ref.shape, 1) == f,
            tile_ref[...].astype(F32), 0.0,
        ),
        axis=1, keepdims=True,
    )
    aimed_a = jnp.broadcast_to(aimed[0:1], (chunk, half))
    aimed_b = jnp.broadcast_to(aimed[1:2], (chunk, half))
    goals = (fx, ahead, behind, fx + ahead - f)

    def tile_copy(k, kind, r, parity):
        at = rows(r * chunk, chunk)
        if kind == DIAGONAL:
            target, landing = (fx if parity else ahead), bent.at[k, at]
        else:
            target, landing = goals[kind], got.at[k, kind, at]
        return pltpu.make_async_remote_copy(
            src_ref=stage.at[k, kind, at], dst_ref=landing,
            send_sem=tile_send.at[k, kind, r], recv_sem=tile_recv.at[k, kind, r],
            device_id={"front": target}, device_id_type=MESH,
        )

    def volume(k):
        s1_copies[k].wait_recv()
        both = jnp.concatenate([s1[k, 0], s1[k, 1]], axis=1)

        @pl.loop(0, chunks)
        def _(r):
            at = rows(r * chunk, chunk)
            pull[at] = mm(ct[at], both).astype(BF)

        @pl.loop(0, chunks)
        def _(r):
            at = rows(r * chunk, chunk)
            change = mm(gf[at], pull[...])
            for m in range(2):
                here = pl.ds(m * half + k * quarter, quarter)
                new = (
                    start[at, here].astype(F32) - change[:, m * quarter : (m + 1) * quarter]
                ).astype(BF)
                vol[at, here] = new
                value[k, at, pl.ds(m * quarter, quarter)] = new

    def contribute(k):
        @pl.loop(0, tile_chunks // 2)
        def _(pair):
            for parity in range(2):
                r = pair * 2 + parity
                at = rows(r * chunk, chunk)
                first = mm(av[1, at], value[k])
                second = mm(av[2, at], value[k])
                for kind in (DIAGONAL, X, Z_ON, Z_BACK):
                    goal = goals[kind].astype(F32)
                    stage[k, kind, at] = jnp.where(
                        aimed_a == goal, first, jnp.where(aimed_b == goal, second, 0.0)
                    ).astype(BF)

                @pl.when(has_ahead)
                def _():
                    tile_copy(k, DIAGONAL, r, parity).start()
                    tile_copy(k, Z_ON, r, parity).start()

                if parity:
                    tile_copy(k, X, r, parity).start()
                else:

                    @pl.when(has_behind)
                    def _():
                        tile_copy(k, Z_BACK, r, parity).start()

    def bend(k):
        @pl.loop(0, tile_chunks // 2)
        def _(pair):
            for parity in range(2):
                r = pair * 2 + parity
                at = rows(r * chunk, chunk)
                kind = Z_BACK if parity else X

                @pl.when(has_behind)
                def _():
                    tile_copy(k, DIAGONAL, r, parity).wait_recv()

                stage[k, kind, at] = (
                    stage[k, kind, at].astype(F32) + bent[k, at].astype(F32)
                ).astype(BF)
                if parity:

                    @pl.when(has_behind)
                    def _():
                        tile_copy(k, Z_BACK, r, parity).start()
                else:
                    tile_copy(k, X, r, parity).start()

    def collect(k):
        @pl.loop(0, tile_chunks)
        def _(r):
            at = rows(r * chunk, chunk)
            total = mm(av[0, at], value[k])
            tile_copy(k, X, r, 0).wait_recv()

            @pl.when(has_behind)
            def _():
                tile_copy(k, Z_ON, r, 0).wait_recv()

            @pl.when(has_ahead)
            def _():
                tile_copy(k, Z_BACK, r, 0).wait_recv()

            for kind in (X, Z_ON, Z_BACK):
                total = total + got[k, kind, at].astype(F32)
            for m in range(2):
                tiles[at, pl.ds(m * half + k * quarter, quarter)] = total[
                    :, m * quarter : (m + 1) * quarter
                ].astype(BF)

    volume(0)
    contribute(0)
    volume(1)
    bend(0)
    contribute(1)

    o3s[b0] = s3[rows(me3 * r3, r3)]
    o2s[b0] = s2[rows(me2 * r2, r2)]
    for k in range(2):
        for m in range(2):
            o1[:, m * half + k * quarter : m * half + (k + 1) * quarter] = s1[
                k, m, rows(me1 * r1, r1)
            ]
    o2_copy.wait_recv()
    o3_copy.wait_recv()
    for m in range(2):
        o2[:, m * half : (m + 1) * half] = o2s[m]
        o3[:, m * half : (m + 1) * half] = o3s[m]

    bend(1)
    collect(0)
    collect(1)

    for copy in copies:
        copy.wait_send()
    for k in range(2):

        @pl.loop(0, tile_chunks)
        def _(r):
            tile_copy(k, X, r, 0).wait_send()

            @pl.when(has_ahead)
            def _():
                tile_copy(k, Z_ON, r, 0).wait_send()
                tile_copy(k, DIAGONAL, r, 0).wait_send()

            @pl.when(has_behind)
            def _():
                tile_copy(k, Z_BACK, r, 0).wait_send()


def hand_over(*refs):
    count = (len(refs) - 2) // 3
    sources, goals, held = refs[:count], refs[count : 2 * count], refs[2 * count : 3 * count]
    in_sem, out_sem = refs[-2:]
    arriving = [
        pltpu.make_async_copy(sources[i], held[i], in_sem.at[i]) for i in range(count)
    ]
    leaving = [
        pltpu.make_async_copy(held[i], goals[i], out_sem.at[i]) for i in range(count)
    ]
    for copy in arriving:
        copy.start()
    for i in range(count):
        arriving[i].wait()
        leaving[i].start()
    for copy in leaving:
        copy.wait()


def local(
    leaf_load, leaf_inverse, leaf_coupling, leaf_rowmap,
    load_first, load_second, load_third,
    inverse_first, inverse_second, inverse_third,
    coupling_first, coupling_second, rowmap_first, rowmap_second,
    surface_coupling, neighbor_tiles,
):
    n = lax.axis_size("front")
    width = lax.axis_size("col")
    fr, panel = leaf_load.shape
    sep = leaf_coupling.shape[0]
    block = leaf_inverse.shape[0]
    tile = surface_coupling.shape[1]
    half, quarter = panel // 2, panel // 4
    r1, r2, r3 = inverse_first.shape[0], inverse_second.shape[0], inverse_third.shape[0]
    vmem = pl.BlockSpec(memory_space=pltpu.VMEM)
    hbm = pl.BlockSpec(memory_space=pl.ANY)

    def v(*shape, dtype=BF):
        return pltpu.VMEM(shape, dtype)

    results = pl.pallas_call(
        functools.partial(kernel, n),
        out_shape=[
            jax.ShapeDtypeStruct(s, BF)
            for s in ((fr, panel), (tile, panel), (r1, panel), (r2, panel), (r3, panel))
        ],
        in_specs=[hbm, vmem, hbm] + [vmem] * 12 + [hbm],
        out_specs=[vmem] * 5,
        scratch_shapes=[
            v(block * width, fr), v(fr, sep), v(fr, panel), v(sep, panel, dtype=F32),
            v(2, 2 * r1, sep), v(4, 2 * r2, sep), v(8, r3, sep),
            v(sep, half), v(sep, half), v(sep, half),
            v(fr, panel), v(sep, fr),
            v(2, sep, quarter), v(2, sep, quarter), v(2, sep, quarter), v(2, sep, quarter),
            v(2, sep, quarter), v(2, sep, quarter), v(2, sep, quarter), v(2, sep, quarter),
            v(sep, half), v(sep, half), v(2, 2, sep, quarter),
            v(2, r3, half), v(2, r2, half), v(fr, half), v(2, fr, half),
            v(*surface_coupling.shape), v(2, 4, tile, half), v(2, 3, tile, half), v(2, tile, half),
            pltpu.SemaphoreType.DMA((64,)), pltpu.SemaphoreType.DMA((64,)),
            pltpu.SemaphoreType.DMA((2, 4, tile // block)),
            pltpu.SemaphoreType.DMA((2, 4, tile // block)),
            pltpu.SemaphoreType.DMA((3,)),
        ],
        compiler_params=pltpu.CompilerParams(
            collective_id=0, has_side_effects=True, vmem_limit_bytes=56 * 1024 * 1024
        ),
        cost_estimate=pl.CostEstimate(
            flops=12 * fr * fr * panel, bytes_accessed=16 * fr * fr, transcendentals=0
        ),
    )(
        leaf_load, leaf_inverse, leaf_coupling, leaf_rowmap,
        load_first, load_second, load_third,
        inverse_first, inverse_second, inverse_third,
        coupling_first, coupling_second, rowmap_first, rowmap_second, neighbor_tiles.T,
        surface_coupling,
    )
    return pl.pallas_call(
        hand_over,
        out_shape=[jax.ShapeDtypeStruct(x.shape, x.dtype) for x in results],
        in_specs=[hbm] * 5,
        out_specs=[hbm] * 5,
        scratch_shapes=[v(*x.shape) for x in results]
        + [pltpu.SemaphoreType.DMA((5,)), pltpu.SemaphoreType.DMA((5,))],
        compiler_params=pltpu.CompilerParams(vmem_limit_bytes=60 * 1024 * 1024),
    )(*results)


def solution(mesh):
    return jax.shard_map(
        local,
        mesh=mesh,
        in_specs=(
            P("front", "col"), P(("front", "col"), None), P("front", None), P("front", None),
            P("front", "col"), P("front", "col"), P("front", "col"),
            P("front", None), P("front", None), P("front", None),
            P(None, "front"), P(None, "front"), P(), P(),
            P("front", None, None), P(),
        ),
        out_specs=(P("front", "col"),) * 5,
        check_vma=False,
    )
```

profile of v0, /device:TPU:0, one launch (start us, length us, event | category | flops | bytes accessed | tf_op | source)
XLA Modules:
  0.0 98.6 jit_solution(15586521363417367999)
XLA Ops:
  0.6 95.2 %shard_map.191 = (bf16[1024,512]{1,0:T(8,128)(2,1)}, bf16[1024,512]{1,0:T(8,128)(2,1)}, bf16[256,512]{1,0:T(8,128)(2,1)}, bf16[128,512]{1,0:T(8,128)(2,1)}, bf16[64,512]{1,0:T(8,128)(2,1)}) custom-call(bf16[1024,512]{1,0:T(8,128)(2,1)} %b_hbm.1, bf16[256,1024]{1,0:T(8,128)(2,1)} %g_ref.1, bf16[512,1024]{1,0:T(8,128)(2,1)} %c_hbm.1, s32[1,512]{1,0:T(1,128)} %map0.1, ...), custom_call_target="tpu_custom_call" | custom-call | flops 6442450944 | bytes 16777216 | tf_op jit(solution)/shard_map/pallas_call | solution.py:438
  95.8 2.8 %shard_map.192 = (bf16[1024,512]{1,0:T(8,128)(2,1)}, bf16[1024,512]{1,0:T(8,128)(2,1)}, bf16[256,512]{1,0:T(8,128)(2,1)}, bf16[128,512]{1,0:T(8,128)(2,1)}, bf16[64,512]{1,0:T(8,128)(2,1)}) custom-call(bf16[1024,512]{1,0:T(8,128)(2,1)} %get-tuple-element.10.refs_0_, bf16[1024,512]{1,0:T(8,128)(2,1)} %get-tuple-element.11.refs_1_, ...), custom_call_target="tpu_custom_call" | custom-call | tf_op jit(solution)/shard_map/pallas_call | solution.py:474
where the time goes:
time: 98.8 us; the launch traced here: 98.6 us
  Pallas kernels  98 us (99%)
    pallas_call x1, Pallas kernels, local(): pl.pallas_call(functools.partial(kernel, n), out_shape=[jax.ShapeDtypeStr...  95.2 us
    pallas_call x1, Pallas kernels, local(): pl.pallas_call(hand_over, out_shape=[jax.ShapeDtypeStruct(x.shape, x.dtyp...  2.76 us

commit v1 on v0

--- a/solution.py
+++ b/solution.py
@@ -70,8 +70,8 @@
         pltpu.make_async_copy(src, dst, load_sem.at[i])
         for i, (src, dst) in enumerate(((b_hbm, b_ref), (c_hbm, c_ref), (a_hbm, av)))
     ]
-    for load in loads:
-        load.start()
+    loads[0].start()
+    loads[1].start()
 
     barrier = pltpu.get_barrier_semaphore()
     for other in (ca, cb):
@@ -91,12 +91,13 @@
     pl.semaphore_wait(barrier, count)
 
     own_rows = rows(c * block, block)
-    g_near = send(g_ref, gf.at[own_rows], col=ca)
     piece = block // 2
     g_far = [
         send(g_ref.at[pl.ds(k * piece, piece)], gf.at[rows(c * block + k * piece, piece)], col=cb)
         for k in range(2)
     ]
+    g_near = send(g_ref, gf.at[own_rows], col=ca)
+    loads[2].start()
 
     lines = lax.broadcasted_iota(jnp.int32, (sep, sep), 0)
 
@@ -249,15 +250,17 @@
     aimed_b = jnp.broadcast_to(aimed[1:2], (chunk, half))
     goals = (fx, ahead, behind, fx + ahead - f)
 
-    def tile_copy(k, kind, r, parity):
-        at = rows(r * chunk, chunk)
+    sub = chunk // 2
+
+    def tile_copy(k, kind, r, parity, h):
+        at = rows(r * chunk + h * sub, sub)
         if kind == DIAGONAL:
             target, landing = (fx if parity else ahead), bent.at[k, at]
         else:
             target, landing = goals[kind], got.at[k, kind, at]
         return pltpu.make_async_remote_copy(
             src_ref=stage.at[k, kind, at], dst_ref=landing,
-            send_sem=tile_send.at[k, kind, r], recv_sem=tile_recv.at[k, kind, r],
+            send_sem=tile_send.at[k, kind, 2 * r + h], recv_sem=tile_recv.at[k, kind, 2 * r + h],
             device_id={"front": target}, device_id_type=MESH,
         )
 
@@ -298,54 +301,61 @@
 
                 @pl.when(has_ahead)
                 def _():
-                    tile_copy(k, DIAGONAL, r, parity).start()
-                    tile_copy(k, Z_ON, r, parity).start()
+                    for kind in (DIAGONAL, Z_ON):
+                        for h in range(2):
+                            tile_copy(k, kind, r, parity, h).start()
 
                 if parity:
-                    tile_copy(k, X, r, parity).start()
+                    for h in range(2):
+                        tile_copy(k, X, r, parity, h).start()
                 else:
 
                     @pl.when(has_behind)
                     def _():
-                        tile_copy(k, Z_BACK, r, parity).start()
+                        for h in range(2):
+                            tile_copy(k, Z_BACK, r, parity, h).start()
 
     def bend(k):
         @pl.loop(0, tile_chunks // 2)
         def _(pair):
             for parity in range(2):
                 r = pair * 2 + parity
-                at = rows(r * chunk, chunk)
                 kind = Z_BACK if parity else X
-
-                @pl.when(has_behind)
-                def _():
-                    tile_copy(k, DIAGONAL, r, parity).wait_recv()
-
-                stage[k, kind, at] = (
-                    stage[k, kind, at].astype(F32) + bent[k, at].astype(F32)
-                ).astype(BF)
-                if parity:
+                for h in range(2):
+                    at = rows(r * chunk + h * sub, sub)
 
                     @pl.when(has_behind)
                     def _():
-                        tile_copy(k, Z_BACK, r, parity).start()
-                else:
-                    tile_copy(k, X, r, parity).start()
+                        tile_copy(k, DIAGONAL, r, parity, h).wait_recv()
+
+                    stage[k, kind, at] = (
+                        stage[k, kind, at].astype(F32) + bent[k, at].astype(F32)
+                    ).astype(BF)
+                    if parity:
+
+                        @pl.when(has_behind)
+                        def _():
+                            tile_copy(k, Z_BACK, r, parity, h).start()
+                    else:
+                        tile_copy(k, X, r, parity, h).start()
 
     def collect(k):
         @pl.loop(0, tile_chunks)
         def _(r):
             at = rows(r * chunk, chunk)
             total = mm(av[0, at], value[k])
-            tile_copy(k, X, r, 0).wait_recv()
+            for h in range(2):
+                tile_copy(k, X, r, 0, h).wait_recv()
 
             @pl.when(has_behind)
             def _():
-                tile_copy(k, Z_ON, r, 0).wait_recv()
+                for h in range(2):
+                    tile_copy(k, Z_ON, r, 0, h).wait_recv()
 
             @pl.when(has_ahead)
             def _():
-                tile_copy(k, Z_BACK, r, 0).wait_recv()
+                for h in range(2):
+                    tile_copy(k, Z_BACK, r, 0, h).wait_recv()
 
             for kind in (X, Z_ON, Z_BACK):
                 total = total + got[k, kind, at].astype(F32)
@@ -383,16 +393,19 @@
 
         @pl.loop(0, tile_chunks)
         def _(r):
-            tile_copy(k, X, r, 0).wait_send()
+            for h in range(2):
+                tile_copy(k, X, r, 0, h).wait_send()
 
             @pl.when(has_ahead)
             def _():
-                tile_copy(k, Z_ON, r, 0).wait_send()
-                tile_copy(k, DIAGONAL, r, 0).wait_send()
+                for h in range(2):
+                    tile_copy(k, Z_ON, r, 0, h).wait_send()
+                    tile_copy(k, DIAGONAL, r, 0, h).wait_send()
 
             @pl.when(has_behind)
             def _():
-                tile_copy(k, Z_BACK, r, 0).wait_send()
+                for h in range(2):
+                    tile_copy(k, Z_BACK, r, 0, h).wait_send()
 
 
 def hand_over(*refs):
@@ -454,8 +467,8 @@
             v(2, r3, half), v(2, r2, half), v(fr, half), v(2, fr, half),
             v(*surface_coupling.shape), v(2, 4, tile, half), v(2, 3, tile, half), v(2, tile, half),
             pltpu.SemaphoreType.DMA((64,)), pltpu.SemaphoreType.DMA((64,)),
-            pltpu.SemaphoreType.DMA((2, 4, tile // block)),
-            pltpu.SemaphoreType.DMA((2, 4, tile // block)),
+            pltpu.SemaphoreType.DMA((2, 4, 2 * tile // block)),
+            pltpu.SemaphoreType.DMA((2, 4, 2 * tile // block)),
             pltpu.SemaphoreType.DMA((3,)),
         ],
         compiler_params=pltpu.CompilerParams(

time: 98.8 us -> 99.4 us (level)
  no operation moved by 1% of the time
where the time goes in v1:
time: 99.4 us; the launch traced here: 99.2 us
  Pallas kernels  98.6 us (99%)
    pallas_call x1, Pallas kernels, local(): pl.pallas_call(functools.partial(kernel, n), out_shape=[jax.ShapeDtypeStr...  95.8 us
    pallas_call x1, Pallas kernels, local(): pl.pallas_call(hand_over, out_shape=[jax.ShapeDtypeStruct(x.shape, x.dtyp...  2.76 us

profile of v1, /device:TPU:0, one launch (start us, length us, event | category | flops | bytes accessed | tf_op | source)
XLA Modules:
  0.0 99.2 jit_solution(14500694601336959009)
XLA Ops:
  0.6 95.8 %shard_map.191 = (bf16[1024,512]{1,0:T(8,128)(2,1)}, bf16[1024,512]{1,0:T(8,128)(2,1)}, bf16[256,512]{1,0:T(8,128)(2,1)}, bf16[128,512]{1,0:T(8,128)(2,1)}, bf16[64,512]{1,0:T(8,128)(2,1)}) custom-call(bf16[1024,512]{1,0:T(8,128)(2,1)} %b_hbm.1, bf16[256,1024]{1,0:T(8,128)(2,1)} %g_ref.1, bf16[512,1024]{1,0:T(8,128)(2,1)} %c_hbm.1, s32[1,512]{1,0:T(1,128)} %map0.1, ...), custom_call_target="tpu_custom_call" | custom-call | flops 6442450944 | bytes 16777216 | tf_op jit(solution)/shard_map/pallas_call | solution.py:451
  96.5 2.8 %shard_map.192 = (bf16[1024,512]{1,0:T(8,128)(2,1)}, bf16[1024,512]{1,0:T(8,128)(2,1)}, bf16[256,512]{1,0:T(8,128)(2,1)}, bf16[128,512]{1,0:T(8,128)(2,1)}, bf16[64,512]{1,0:T(8,128)(2,1)}) custom-call(bf16[1024,512]{1,0:T(8,128)(2,1)} %get-tuple-element.10.refs_0_, bf16[1024,512]{1,0:T(8,128)(2,1)} %get-tuple-element.11.refs_1_, ...), custom_call_target="tpu_custom_call" | custom-call | tf_op jit(solution)/shard_map/pallas_call | solution.py:487

commit v2 on v0

--- a/solution.py
+++ b/solution.py
@@ -357,8 +357,8 @@
     volume(0)
     contribute(0)
     volume(1)
+    contribute(1)
     bend(0)
-    contribute(1)
 
     o3s[b0] = s3[rows(me3 * r3, r3)]
     o2s[b0] = s2[rows(me2 * r2, r2)]

time: 98.8 us -> 98.8 us (level)
  no operation moved by 1% of the time
where the time goes in v2:
time: 98.8 us; the launch traced here: 98.6 us
  Pallas kernels  98 us (99%)
    pallas_call x1, Pallas kernels, local(): pl.pallas_call(functools.partial(kernel, n), out_shape=[jax.ShapeDtypeStr...  95.2 us
    pallas_call x1, Pallas kernels, local(): pl.pallas_call(hand_over, out_shape=[jax.ShapeDtypeStruct(x.shape, x.dtyp...  2.76 us

profile of v2, /device:TPU:0, one launch (start us, length us, event | category | flops | bytes accessed | tf_op | source)
XLA Modules:
  0.0 98.6 jit_solution(8598837725173358157)
XLA Ops:
  0.6 95.2 %shard_map.191 = (bf16[1024,512]{1,0:T(8,128)(2,1)}, bf16[1024,512]{1,0:T(8,128)(2,1)}, bf16[256,512]{1,0:T(8,128)(2,1)}, bf16[128,512]{1,0:T(8,128)(2,1)}, bf16[64,512]{1,0:T(8,128)(2,1)}) custom-call(bf16[1024,512]{1,0:T(8,128)(2,1)} %b_hbm.1, bf16[256,1024]{1,0:T(8,128)(2,1)} %g_ref.1, bf16[512,1024]{1,0:T(8,128)(2,1)} %c_hbm.1, s32[1,512]{1,0:T(1,128)} %map0.1, ...), custom_call_target="tpu_custom_call" | custom-call | flops 6442450944 | bytes 16777216 | tf_op jit(solution)/shard_map/pallas_call | solution.py:438
  95.8 2.8 %shard_map.192 = (bf16[1024,512]{1,0:T(8,128)(2,1)}, bf16[1024,512]{1,0:T(8,128)(2,1)}, bf16[256,512]{1,0:T(8,128)(2,1)}, bf16[128,512]{1,0:T(8,128)(2,1)}, bf16[64,512]{1,0:T(8,128)(2,1)}) custom-call(bf16[1024,512]{1,0:T(8,128)(2,1)} %get-tuple-element.10.refs_0_, bf16[1024,512]{1,0:T(8,128)(2,1)} %get-tuple-element.11.refs_1_, ...), custom_call_target="tpu_custom_call" | custom-call | tf_op jit(solution)/shard_map/pallas_call | solution.py:474
